TPU v7x, 32 devices: a whole 2x2x4 slice. The times are simulated.
32 devices in a mesh: row: 8 (over z, core), col: 4 (over y, x).
Axes of the slice: x: 2, y: 2, z: 4, core: 2. Of those that a mesh axis runs over, the one named last changes fastest.
Arguments:
- left_prop: float32 [8, 8, 2, 512, 512], P('row', None, None, 'col'), may hold values from -0.1875 to 0.1875
- vertex: float32 [8, 2, 512, 512], P(None, None, ('row', 'col')), may hold values from -5 to 5
- right_prop: float32 [8, 8, 2, 512, 512], P(None, 'col', None, None, 'row'), may hold values from -0.1875 to 0.1875
- insertions: int32 [3], replicated, may hold values from 0 to 7
- window_start: int32 [2], replicated, may hold values from 0 to 255
Outputs:
- correlator: float32 [8, 8, 2, 512, 512], P('row', 'col')
Inputs may be any that keep to these rules, and one draw needn't show every extreme that they name: `insertions`: repeats may occur.
All inputs are finite; a program needn't handle non-finite values.
Results may differ from a plain program's by a relative error of at most 0.0001.
Values sent between devices are 32-bit elements; how exact they have to be, the bound alone decides.
A program may use at most 128 MiB of HBM per device.

v0:
```python
import functools

import jax
import jax.numpy as jnp
from jax import lax
from jax.experimental import pallas as pl
from jax.experimental.pallas import tpu as pltpu
from jax.sharding import PartitionSpec as P

NS = 8
LT = 256
MESH = pl.DeviceIdType.MESH
F32 = jnp.float32
BF16 = jnp.bfloat16


def choose_kernel(ins, left_sign, right_sign, left_ref, vertex_ref, right_ref, l_ref, v_ref, r_ref):
    k = pl.program_id(0)
    l_ref[0] = left_ref[0, 0] * left_sign[k]
    v_ref[0] = vertex_ref[0]
    for u in range(right_ref.shape[1]):
        for part in range(2):
            r_ref[0, part, u] = right_ref[0, u, part] * right_sign[k, u]


def choose(left_prop, vertex, right_t, insertions, left_sign, right_sign):
    count = insertions.shape[0]
    _, _, _, lrows, m = left_prop.shape
    vrows = vertex.shape[2]
    sinks, cols = right_t.shape[1], right_t.shape[3]
    return pl.pallas_call(
        choose_kernel,
        grid_spec=pltpu.PrefetchScalarGridSpec(
            num_scalar_prefetch=3,
            grid=(count,),
            in_specs=[
                pl.BlockSpec((1, 1, 2, lrows, m), lambda k, i, *_: (0, i[k], 0, 0, 0)),
                pl.BlockSpec((1, 2, vrows, m), lambda k, i, *_: (i[k], 0, 0, 0)),
                pl.BlockSpec((1, sinks, 2, cols, m), lambda k, i, *_: (i[k], 0, 0, 0, 0)),
            ],
            out_specs=[
                pl.BlockSpec((1, 2, lrows, m), lambda k, *_: (k, 0, 0, 0)),
                pl.BlockSpec((1, 2, vrows, m), lambda k, *_: (k, 0, 0, 0)),
                pl.BlockSpec((1, 2, sinks, cols, m), lambda k, *_: (k, 0, 0, 0, 0)),
            ],
        ),
        out_shape=[
            jax.ShapeDtypeStruct((count, 2, lrows, m), F32),
            jax.ShapeDtypeStruct((count, 2, vrows, m), F32),
            jax.ShapeDtypeStruct((count, 2, sinks, cols, m), F32),
        ],
    )(insertions, left_sign, right_sign, left_prop, vertex, right_t)


def halves(x):
    high = x.astype(BF16)
    return high, (x - high.astype(F32)).astype(BF16)


def dot_nn(a, b):
    return lax.dot_general(a, b, (((1,), (0,)), ((), ())), preferred_element_type=F32)


def dot_nt(a, b):
    return lax.dot_general(a, b, (((1,), (1,)), ((), ())), preferred_element_type=F32)


def main_kernel(
    nz, l_ref, v_ref, r_ref, out_ref,
    v_all, r_all, lv_all, lv_high, lv_low, acc,
    v_send_z, v_send, v_recv, r_send, r_recv, lv_send, lv_recv,
):
    count, _, lrows, m = l_ref.shape
    vrows = v_ref.shape[2]
    sinks = out_ref.shape[1]
    rrows = r_ref.shape[1]
    half = rrows // 2
    cols = half // sinks
    ncol = 4
    row, c = lax.axis_index("row"), lax.axis_index("col")
    z, h = row // 2, lax.rem(row, 2)
    cx = c + 1 - 2 * lax.rem(c, 2)
    cy = lax.rem(c + 2, ncol)
    cd = lax.rem(cx + 2, ncol)
    sib = (2 * z + 1 - h, c)
    to_x, to_y = (row, cx), (row, cy)
    up, down = (row + 2, c), (row - 2, c)

    barrier = pltpu.get_barrier_semaphore()
    for dz in range(1, nz):
        pl.semaphore_signal(barrier, inc=1, device_id=(2 * lax.rem(z + dz, nz) + h, c), device_id_type=MESH)
    for dev in (sib, to_x, to_y):
        pl.semaphore_signal(barrier, inc=1, device_id=dev, device_id_type=MESH)
    pl.semaphore_wait(barrier, nz - 1 + 3)

    pending = []

    def send(src, dst, ssem, rsem, dev, when=None):
        def make():
            return pltpu.make_async_remote_copy(
                src_ref=src(), dst_ref=dst(), send_sem=ssem(), recv_sem=rsem(), device_id=dev, device_id_type=MESH
            )

        if when is None:
            make().start()
        else:
            pl.when(when)(lambda: make().start())
        pending.append((when, make))

    def arrived(dst, rsem):
        pltpu.make_async_remote_copy(
            src_ref=dst, dst_ref=dst, send_sem=v_send_z.at[0], recv_sem=rsem, device_id=sib, device_id_type=MESH
        ).wait_recv()

    def v_slot(zs, hs, cs):
        return v_all.at[:, :, pl.ds(pl.multiple_of(((2 * zs + hs) * ncol + cs) * vrows, vrows), vrows), :]

    def v_sem(zs, hs, cs):
        return v_recv.at[(2 * zs + hs) * ncol + cs]

    for dz in range(1, nz):
        send(
            lambda: v_ref, lambda: v_slot(z, h, c), lambda dz=dz: v_send_z.at[dz], lambda: v_sem(z, h, c),
            (2 * lax.rem(z + dz, nz) + h, c),
        )

    def v_pass(kind, j, mm, src, zs, cs, dev):
        send(src, lambda: v_slot(zs, h, cs), lambda: v_send.at[kind, j, mm], lambda: v_sem(zs, h, cs), dev)

    for mm in range(nz):
        zs = lax.rem(z + mm, nz)
        if mm == 0:
            src = lambda: v_ref
        else:
            src = lambda zs=zs: v_slot(zs, h, c)
            arrived(v_slot(zs, h, c), v_sem(zs, h, c))
        v_pass(0, 0, mm, src, zs, c, to_x)
        v_pass(1, 0, mm, src, zs, c, to_y)
        v_pass(2, 0, mm, src, zs, c, sib)
    v_all[:, :, pl.ds(pl.multiple_of((row * ncol + c) * vrows, vrows), vrows), :] = v_ref[...]

    def r_pass(kind, zs, k, src, dev, when=None):
        send(
            src, lambda: r_all.at[2 * zs + h, k], lambda: r_send.at[kind, zs, k], lambda: r_recv.at[2 * zs + h, k],
            dev, when,
        )

    has_up, has_down = z < nz - 1, z > 0
    for k in range(count):
        src = lambda k=k: r_ref.at[k]
        r_pass(0, z, k, src, up, has_up)
        r_pass(1, z, k, src, down, has_down)
    for k in range(count):
        r_pass(2, z, k, lambda k=k: r_ref.at[k], sib)
    r_all[row] = r_ref[...]

    hops = {}
    for d in range(1, nz):
        low_ok, high_ok = z - d >= 0, z + d < nz
        hops[d] = (
            (0, up, z - d, low_ok, jnp.logical_and(low_ok, has_up)),
            (1, down, z + d, high_ok, jnp.logical_and(high_ok, has_down)),
        )

    def r_step(d):
        for k in range(count):
            for kind, toward, zs, ok, onward in hops[d]:
                src = lambda zs=zs, k=k: r_all.at[2 * zs + h, k]

                @pl.when(ok)
                def _(zs=zs, k=k, src=src):
                    arrived(src(), r_recv.at[2 * zs + h, k])

                if d < nz - 1:
                    r_pass(kind, zs, k, src, toward, onward)
                r_pass(2, zs, k, src, sib, ok)

    for mm in range(nz):
        zs = lax.rem(z + mm, nz)
        arrived(v_slot(zs, h, cx), v_sem(zs, h, cx))
        src = lambda zs=zs: v_slot(zs, h, cx)
        if mm < nz // 2:
            v_pass(1, 1, mm, src, zs, cx, to_y)
        v_pass(2, 1, mm, src, zs, cx, sib)
        arrived(v_slot(zs, h, cy), v_sem(zs, h, cy))
        src = lambda zs=zs: v_slot(zs, h, cy)
        if mm >= nz // 2:
            v_pass(0, 1, mm, src, zs, cy, to_x)
        v_pass(2, 2, mm, src, zs, cy, sib)
    for mm in range(nz):
        zs = lax.rem(z + mm, nz)
        arrived(v_slot(zs, h, cd), v_sem(zs, h, cd))
        v_pass(2, 3, mm, lambda zs=zs: v_slot(zs, h, cd), zs, cd, sib)
    for mm in range(nz):
        zs = lax.rem(z + mm, nz)
        for cs in (c, cx, cy, cd):
            arrived(v_slot(zs, 1 - h, cs), v_sem(zs, 1 - h, cs))

    def lv_piece(cs, k, part):
        return lv_all.at[cs, k, part]

    def lv_pass(kind, fwd, k, part, cs, dev):
        send(
            lambda: lv_piece(cs, k, part), lambda: lv_piece(cs, k, part),
            lambda: lv_send.at[kind, fwd, k, part], lambda: lv_recv.at[cs, k, part], dev,
        )

    def split_lv(cs, k, part):
        high, low = halves(lv_all[cs, k, part])
        at = pl.ds(pl.multiple_of(part * m + cs * lrows, lrows), lrows)
        lv_high[k, at, :] = high
        lv_low[k, at, :] = low

    for k in range(count):
        xh, xl = halves(l_ref[k].reshape(2 * lrows, m))
        prods = []
        for part in range(2):
            vh, vl = halves(v_all[k, part])
            prods.append(dot_nn(xh, vh) + dot_nn(xl, vh) + dot_nn(xh, vl))
        lv_all[c, k, 0] = prods[0][:lrows] - prods[1][lrows:]
        lv_all[c, k, 1] = prods[1][:lrows] + prods[0][lrows:]
        for part in range(2):
            lv_pass(0, 0, k, part, c, to_x)
            lv_pass(1, 0, k, part, c, to_y)

    r_step(1)

    for k in range(count):
        for part in range(2):
            split_lv(c, k, part)
    for k in range(count):
        for part in range(2):
            arrived(lv_piece(cx, k, part), lv_recv.at[cx, k, part])
            if part == 0:
                lv_pass(1, 1, k, part, cx, to_y)
            arrived(lv_piece(cy, k, part), lv_recv.at[cy, k, part])
            if part == 1:
                lv_pass(0, 1, k, part, cy, to_x)
            split_lv(cx, k, part)
            split_lv(cy, k, part)
    for d in range(2, nz - 1):
        r_step(d)
    for k in range(count):
        for part in range(2):
            arrived(lv_piece(cd, k, part), lv_recv.at[cd, k, part])
            split_lv(cd, k, part)

    def chip(i, carry):
        d = (i + 1) // 2
        q = z + d * (1 - 2 * lax.rem(i, 2))
        if nz > 2:
            pl.when(i == 2 * (nz - 1) - 1)(lambda: r_step(nz - 1))

        @pl.when(jnp.logical_and(q >= 0, q < nz))
        def _():
            for k in range(count):
                arrived(r_all.at[2 * q + 1 - h, k], r_recv.at[2 * q + 1 - h, k])

            def one(j, carry):
                for k in range(count):
                    yh, yl = halves(r_all[2 * q + j, k])
                    for part in range(2):
                        at = pl.ds(part * m, m)
                        p = (
                            dot_nt(lv_high[k, at, :], yh)
                            + dot_nt(lv_low[k, at, :], yh)
                            + dot_nt(lv_high[k, at, :], yl)
                        )
                        if k == 0:
                            acc[j, at, :] = p
                        else:
                            acc[j, at, :] += p
                return carry

            lax.fori_loop(0, 2, one, 0)
            real, imag = [], []
            for j in range(2):
                real.append(acc[j, pl.ds(0, m), pl.ds(0, half)] - acc[j, pl.ds(m, m), pl.ds(half, half)])
                imag.append(acc[j, pl.ds(0, m), pl.ds(half, half)] + acc[j, pl.ds(m, m), pl.ds(0, half)])
            for u in range(sinks):
                cut = slice(u * cols, (u + 1) * cols)
                out_ref[q, u, 0] = jnp.concatenate([real[0][:, cut], real[1][:, cut]], axis=1)
                out_ref[q, u, 1] = jnp.concatenate([imag[0][:, cut], imag[1][:, cut]], axis=1)

        return carry

    lax.fori_loop(0, 2 * nz - 1, chip, 0)

    for when, make in pending:
        if when is None:
            make().wait_send()
        else:
            pl.when(when)(lambda make=make: make().wait_send())


def exchange_and_contract(nrow, ncol, chosen_left, chosen_vertex, chosen_right):
    count, _, lrows, m = chosen_left.shape
    vrows = chosen_vertex.shape[2]
    sinks, cols = chosen_right.shape[2], chosen_right.shape[3]
    rrows = 2 * sinks * cols
    nz = nrow // 2
    dma = pltpu.SemaphoreType.DMA
    vmem = pl.BlockSpec(memory_space=pltpu.VMEM)
    return pl.pallas_call(
        functools.partial(main_kernel, nz),
        out_shape=jax.ShapeDtypeStruct((nz, sinks, 2, m, 2 * cols), F32),
        in_specs=[vmem, vmem, vmem],
        out_specs=vmem,
        scratch_shapes=[
            pltpu.VMEM((count, 2, nrow * ncol * vrows, m), F32),
            pltpu.VMEM((nrow, count, rrows, m), F32),
            pltpu.VMEM((ncol, count, 2, lrows, m), F32),
            pltpu.VMEM((count, 2 * m, m), BF16),
            pltpu.VMEM((count, 2 * m, m), BF16),
            pltpu.VMEM((2, 2 * m, rrows), F32),
            dma((nz,)),
            dma((3, 4, nz)),
            dma((nrow * ncol,)),
            dma((3, nz, count)),
            dma((nrow, count)),
            dma((2, 2, count, 2)),
            dma((ncol, count, 2)),
        ],
        compiler_params=pltpu.CompilerParams(
            collective_id=0, has_side_effects=True, vmem_limit_bytes=58 * 1024 * 1024
        ),
    )(chosen_left, chosen_vertex, chosen_right.reshape(count, rrows, m))


def complex_product(first, second):
    highest = lax.Precision.HIGHEST
    first_re, first_im = first[..., 0, :, :], first[..., 1, :, :]
    second_re, second_im = second[..., 0, :, :], second[..., 1, :, :]
    real_part = jnp.matmul(first_re, second_re, precision=highest) - jnp.matmul(first_im, second_im, precision=highest)
    imag_part = jnp.matmul(first_re, second_im, precision=highest) + jnp.matmul(first_im, second_re, precision=highest)
    return jnp.stack([real_part, imag_part], axis=-3)


def pick(array, insertions, axis):
    parts = [lax.dynamic_index_in_dim(array, insertions[k], axis, keepdims=True) for k in range(insertions.shape[0])]
    return jnp.concatenate(parts, axis=axis)


def general(left_prop, vertex, right_prop, insertions, left_sign, right_sign):
    chosen_left = pick(left_prop, insertions, 1) * left_sign[:, :, None, None, None]
    chosen_right = pick(right_prop, insertions, 0) * right_sign[:, :, None, None, None]
    vertex_full = lax.all_gather(pick(vertex, insertions, 0), ("row", "col"), axis=2, tiled=True)
    through = complex_product(chosen_left, vertex_full[None])
    through = lax.all_gather(through, "col", axis=3, tiled=True)
    right_full = lax.all_gather(chosen_right, "row", axis=4, tiled=True)
    summed = complex_product(through[:, 0, None], right_full[0][None])
    for k in range(1, insertions.shape[0]):
        summed = summed + complex_product(through[:, k, None], right_full[k][None])
    return summed


def per_device(nrow, ncol, left_prop, vertex, right_prop, insertions, window_start):
    source_count = left_prop.shape[0]
    sink_count = right_prop.shape[1]
    source_slots = lax.axis_index("row") * source_count + jnp.arange(source_count, dtype=jnp.int32)
    sink_slots = lax.axis_index("col") * sink_count + jnp.arange(sink_count, dtype=jnp.int32)
    slice_times = insertions * (LT // NS)
    source_times = (window_start[0] + source_slots) % LT
    sink_times = (window_start[1] + sink_slots) % LT
    left_sign = jnp.where(slice_times[None, :] < source_times[:, None], -1.0, 1.0).astype(F32)
    right_sign = jnp.where(sink_times[None, :] < slice_times[:, None], -1.0, 1.0).astype(F32)
    lrows, m = left_prop.shape[3:]
    fits = (
        source_count == 1 and ncol == 4 and nrow % 2 == 0 and nrow >= 4 and vertex.shape[2] % 8 == 0
        and lrows % 16 == 0 and m % 128 == 0 and 2 * right_prop.shape[4] == 128
        and right_prop.shape[1] * right_prop.shape[4] == 128
    )
    if not fits:
        return general(left_prop, vertex, right_prop, insertions, left_sign, right_sign)
    chosen = choose(
        left_prop, vertex, jnp.swapaxes(right_prop, 3, 4), insertions, left_sign[0], right_sign
    )
    blocks = exchange_and_contract(nrow, ncol, *chosen)
    nz, sinks, _, _, width = blocks.shape
    return jnp.transpose(blocks, (1, 2, 3, 0, 4)).reshape(1, sinks, 2, m, nz * width)


def solution(mesh):
    return jax.shard_map(
        functools.partial(per_device, mesh.shape["row"], mesh.shape["col"]),
        mesh=mesh,
        in_specs=(
            P("row", None, None, "col", None),
            P(None, None, ("row", "col"), None),
            P(None, "col", None, None, "row"),
            P(),
            P(),
        ),
        out_specs=P("row", "col", None, None, None),
        check_vma=False,
    )
```

profile of v0, /device:TPU:1, one launch (start us, length us, event | category | flops | bytes accessed | tf_op | source)
XLA Modules:
  0.0 158.2 jit_solution(11279512163716469621)
XLA Ops:
  0.0 0.7 broadcast_multiply_fusion
  0.7 1.3 fusion.1
  2.6 0.7 and_select_fusion
  3.3 1.2 compare_select_fusion.3.left_sign
  4.5 0.6 compare_select_fusion.2.right_sign
  5.2 5.2 %shard_map.55 = (f32[3,2,128,512]{3,2,1,0:T(8,128)}, f32[3,2,16,512]{3,2,1,0:T(8,128)}, f32[3,2,2,64,512]{4,3,2,1,0:T(8,128)}) custom-call(s32[3]{0:T(128)} %ins.1, f32[3]{0:T(128)} %compare_select_fusion.3.left_sign, f32[3,2]{1,0:T(4,128)} %compare_select_fusion.2.right_sign, f32[1,8,2,128,512]{4,3,2,1,0:T(8,128)} %left_ref.1, ...), custom_call_target="tpu_custom_call" | custom-call | tf_op jit(solution)/shard_map/pallas_call | solution.py:31
  10.4 137.3 %shard_map.56 = f32[4,2,2,512,128]{4,3,2,1,0:T(8,128)} custom-call(f32[3,2,128,512]{3,2,1,0:T(8,128)} %get-tuple-element.8.l_ref, f32[3,2,16,512]{3,2,1,0:T(8,128)} %get-tuple-element.9.v_ref, f32[3,256,512]{2,1,0:T(8,128)} %bitcast.10), custom_call_target="tpu_custom_call" | custom-call | tf_op jit(solution)/shard_map/pallas_call | solution.py:304
  147.7 5.3 %copy.6 = f32[2,2,512,4,128]{2,4,3,1,0:T(8,128)} copy(f32[2,2,512,4,128]{4,2,1,0,3:T(8,128)} %bitcast.7) | data formatting | bytes 8388608 | tf_op jit(solution)/shard_map/transpose | solution.py:380
  153.0 5.2 %copy.7 = f32[1,2,2,512,512]{4,3,2,1,0:T(8,128)} copy(f32[1,2,2,512,512]{3,4,2,1,0:T(8,128)} %bitcast.8) | data formatting | bytes 8388608 | tf_op jit(solution)/shard_map/reshape | solution.py:380
where the time goes:
time: 159 us; the launch traced here: 158 us
  Pallas kernels  143 us (90%)
  local copies, waits for them, and re-layouts  11.8 us (7%)
  other arithmetic  3.18 us (2%)
    pallas_call x1, Pallas kernels, exchange_and_contract(): pl.pallas_call(functools.partial(main_kernel, nz), out_shape=jax.ShapeDty...  137 us
    transpose x1, local copies, waits for them, and re-layouts, per_device(): jnp.transpose(blocks, (1, 2, 3, 0, 4)).reshape(1, sinks, 2, m, nz * width)  5.25 us
    reshape x1, local copies, waits for them, and re-layouts, per_device(): jnp.transpose(blocks, (1, 2, 3, 0, 4)).reshape(1, sinks, 2, m, nz * width)  5.22 us
    pallas_call x1, Pallas kernels, choose(): pl.pallas_call(choose_kernel, grid_spec=pltpu.PrefetchScalarGridSpec(num_...  5.21 us

commit v1 on v0

--- a/solution.py
+++ b/solution.py
@@ -14,16 +14,21 @@
 BF16 = jnp.bfloat16
 
 
-def choose_kernel(ins, left_sign, right_sign, left_ref, vertex_ref, right_ref, l_ref, v_ref, r_ref):
+def choose_kernel(ins, start, left_ref, vertex_ref, right_ref, l_ref, v_ref, r_ref):
     k = pl.program_id(0)
-    l_ref[0] = left_ref[0, 0] * left_sign[k]
+    sinks = right_ref.shape[1]
+    slice_time = ins[k] * (LT // NS)
+    source_time = lax.rem(start[0] + lax.axis_index("row"), LT)
+    l_ref[0] = left_ref[0, 0] * jnp.where(slice_time < source_time, -1.0, 1.0).astype(F32)
     v_ref[0] = vertex_ref[0]
-    for u in range(right_ref.shape[1]):
-        for part in range(2):
-            r_ref[0, part, u] = right_ref[0, u, part] * right_sign[k, u]
-
-
-def choose(left_prop, vertex, right_t, insertions, left_sign, right_sign):
+    for u in range(sinks):
+        sink_time = lax.rem(start[1] + lax.axis_index("col") * sinks + u, LT)
+        sign = jnp.where(sink_time < slice_time, -1.0, 1.0).astype(F32)
+        for part in range(2):
+            r_ref[0, part, u] = right_ref[0, u, part] * sign
+
+
+def choose(left_prop, vertex, right_t, insertions, window_start):
     count = insertions.shape[0]
     _, _, _, lrows, m = left_prop.shape
     vrows = vertex.shape[2]
@@ -31,7 +36,7 @@
     return pl.pallas_call(
         choose_kernel,
         grid_spec=pltpu.PrefetchScalarGridSpec(
-            num_scalar_prefetch=3,
+            num_scalar_prefetch=2,
             grid=(count,),
             in_specs=[
                 pl.BlockSpec((1, 1, 2, lrows, m), lambda k, i, *_: (0, i[k], 0, 0, 0)),
@@ -49,7 +54,7 @@
             jax.ShapeDtypeStruct((count, 2, vrows, m), F32),
             jax.ShapeDtypeStruct((count, 2, sinks, cols, m), F32),
         ],
-    )(insertions, left_sign, right_sign, left_prop, vertex, right_t)
+    )(insertions, window_start, left_prop, vertex, right_t)
 
 
 def halves(x):
@@ -124,6 +129,20 @@
             (2 * lax.rem(z + dz, nz) + h, c),
         )
 
+    def r_pass(kind, zs, k, src, dev, when=None):
+        send(
+            src, lambda: r_all.at[2 * zs + h, k], lambda: r_send.at[kind, zs, k], lambda: r_recv.at[2 * zs + h, k],
+            dev, when,
+        )
+
+    has_up, has_down = z < nz - 1, z > 0
+
+    def r_own(k):
+        r_pass(0, z, k, lambda: r_ref.at[k], up, has_up)
+        r_pass(1, z, k, lambda: r_ref.at[k], down, has_down)
+
+    r_own(0)
+
     def v_pass(kind, j, mm, src, zs, cs, dev):
         send(src, lambda: v_slot(zs, h, cs), lambda: v_send.at[kind, j, mm], lambda: v_sem(zs, h, cs), dev)
 
@@ -139,17 +158,8 @@
         v_pass(2, 0, mm, src, zs, c, sib)
     v_all[:, :, pl.ds(pl.multiple_of((row * ncol + c) * vrows, vrows), vrows), :] = v_ref[...]
 
-    def r_pass(kind, zs, k, src, dev, when=None):
-        send(
-            src, lambda: r_all.at[2 * zs + h, k], lambda: r_send.at[kind, zs, k], lambda: r_recv.at[2 * zs + h, k],
-            dev, when,
-        )
-
-    has_up, has_down = z < nz - 1, z > 0
-    for k in range(count):
-        src = lambda k=k: r_ref.at[k]
-        r_pass(0, z, k, src, up, has_up)
-        r_pass(1, z, k, src, down, has_down)
+    for k in range(1, count):
+        r_own(k)
     for k in range(count):
         r_pass(2, z, k, lambda k=k: r_ref.at[k], sib)
     r_all[row] = r_ref[...]
@@ -162,8 +172,8 @@
             (1, down, z + d, high_ok, jnp.logical_and(high_ok, has_down)),
         )
 
-    def r_step(d):
-        for k in range(count):
+    def r_step(d, pieces=range(count)):
+        for k in pieces:
             for kind, toward, zs, ok, onward in hops[d]:
                 src = lambda zs=zs, k=k: r_all.at[2 * zs + h, k]
 
@@ -248,16 +258,20 @@
     def chip(i, carry):
         d = (i + 1) // 2
         q = z + d * (1 - 2 * lax.rem(i, 2))
-        if nz > 2:
-            pl.when(i == 2 * (nz - 1) - 1)(lambda: r_step(nz - 1))
 
         @pl.when(jnp.logical_and(q >= 0, q < nz))
         def _():
             for k in range(count):
-                arrived(r_all.at[2 * q + 1 - h, k], r_recv.at[2 * q + 1 - h, k])
-
-            def one(j, carry):
-                for k in range(count):
+                if nz > 2:
+                    pl.when(d == nz - 1)(lambda k=k: r_step(nz - 1, [k]))
+
+                def one(n, carry, k=k):
+                    j = h + n * (1 - 2 * h)
+
+                    @pl.when(n == 1)
+                    def _():
+                        arrived(r_all.at[2 * q + j, k], r_recv.at[2 * q + j, k])
+
                     yh, yl = halves(r_all[2 * q + j, k])
                     for part in range(2):
                         at = pl.ds(part * m, m)
@@ -270,17 +284,18 @@
                             acc[j, at, :] = p
                         else:
                             acc[j, at, :] += p
-                return carry
-
-            lax.fori_loop(0, 2, one, 0)
+                    return carry
+
+                lax.fori_loop(0, 2, one, 0)
             real, imag = [], []
             for j in range(2):
                 real.append(acc[j, pl.ds(0, m), pl.ds(0, half)] - acc[j, pl.ds(m, m), pl.ds(half, half)])
                 imag.append(acc[j, pl.ds(0, m), pl.ds(half, half)] + acc[j, pl.ds(m, m), pl.ds(0, half)])
+            lanes = pl.ds(pl.multiple_of(q * 2 * cols, 2 * cols), 2 * cols)
             for u in range(sinks):
                 cut = slice(u * cols, (u + 1) * cols)
-                out_ref[q, u, 0] = jnp.concatenate([real[0][:, cut], real[1][:, cut]], axis=1)
-                out_ref[q, u, 1] = jnp.concatenate([imag[0][:, cut], imag[1][:, cut]], axis=1)
+                out_ref[0, u, 0, :, lanes] = jnp.concatenate([real[0][:, cut], real[1][:, cut]], axis=1)
+                out_ref[0, u, 1, :, lanes] = jnp.concatenate([imag[0][:, cut], imag[1][:, cut]], axis=1)
 
         return carry
 
@@ -303,7 +318,7 @@
     vmem = pl.BlockSpec(memory_space=pltpu.VMEM)
     return pl.pallas_call(
         functools.partial(main_kernel, nz),
-        out_shape=jax.ShapeDtypeStruct((nz, sinks, 2, m, 2 * cols), F32),
+        out_shape=jax.ShapeDtypeStruct((1, sinks, 2, m, nrow * cols), F32),
         in_specs=[vmem, vmem, vmem],
         out_specs=vmem,
         scratch_shapes=[
@@ -322,7 +337,7 @@
             dma((ncol, count, 2)),
         ],
         compiler_params=pltpu.CompilerParams(
-            collective_id=0, has_side_effects=True, vmem_limit_bytes=58 * 1024 * 1024
+            collective_id=0, has_side_effects=True, vmem_limit_bytes=48 * 1024 * 1024
         ),
     )(chosen_left, chosen_vertex, chosen_right.reshape(count, rrows, m))
 
@@ -341,7 +356,16 @@
     return jnp.concatenate(parts, axis=axis)
 
 
-def general(left_prop, vertex, right_prop, insertions, left_sign, right_sign):
+def general(left_prop, vertex, right_prop, insertions, window_start):
+    source_count = left_prop.shape[0]
+    sink_count = right_prop.shape[1]
+    source_slots = lax.axis_index("row") * source_count + jnp.arange(source_count, dtype=jnp.int32)
+    sink_slots = lax.axis_index("col") * sink_count + jnp.arange(sink_count, dtype=jnp.int32)
+    slice_times = insertions * (LT // NS)
+    source_times = (window_start[0] + source_slots) % LT
+    sink_times = (window_start[1] + sink_slots) % LT
+    left_sign = jnp.where(slice_times[None, :] < source_times[:, None], -1.0, 1.0).astype(F32)
+    right_sign = jnp.where(sink_times[None, :] < slice_times[:, None], -1.0, 1.0).astype(F32)
     chosen_left = pick(left_prop, insertions, 1) * left_sign[:, :, None, None, None]
     chosen_right = pick(right_prop, insertions, 0) * right_sign[:, :, None, None, None]
     vertex_full = lax.all_gather(pick(vertex, insertions, 0), ("row", "col"), axis=2, tiled=True)
@@ -356,14 +380,6 @@
 
 def per_device(nrow, ncol, left_prop, vertex, right_prop, insertions, window_start):
     source_count = left_prop.shape[0]
-    sink_count = right_prop.shape[1]
-    source_slots = lax.axis_index("row") * source_count + jnp.arange(source_count, dtype=jnp.int32)
-    sink_slots = lax.axis_index("col") * sink_count + jnp.arange(sink_count, dtype=jnp.int32)
-    slice_times = insertions * (LT // NS)
-    source_times = (window_start[0] + source_slots) % LT
-    sink_times = (window_start[1] + sink_slots) % LT
-    left_sign = jnp.where(slice_times[None, :] < source_times[:, None], -1.0, 1.0).astype(F32)
-    right_sign = jnp.where(sink_times[None, :] < slice_times[:, None], -1.0, 1.0).astype(F32)
     lrows, m = left_prop.shape[3:]
     fits = (
         source_count == 1 and ncol == 4 and nrow % 2 == 0 and nrow >= 4 and vertex.shape[2] % 8 == 0
@@ -371,13 +387,9 @@
         and right_prop.shape[1] * right_prop.shape[4] == 128
     )
     if not fits:
-        return general(left_prop, vertex, right_prop, insertions, left_sign, right_sign)
-    chosen = choose(
-        left_prop, vertex, jnp.swapaxes(right_prop, 3, 4), insertions, left_sign[0], right_sign
-    )
-    blocks = exchange_and_contract(nrow, ncol, *chosen)
-    nz, sinks, _, _, width = blocks.shape
-    return jnp.transpose(blocks, (1, 2, 3, 0, 4)).reshape(1, sinks, 2, m, nz * width)
+        return general(left_prop, vertex, right_prop, insertions, window_start)
+    chosen = choose(left_prop, vertex, jnp.swapaxes(right_prop, 3, 4), insertions, window_start)
+    return exchange_and_contract(nrow, ncol, *chosen)
 
 
 def solution(mesh):

time: 159 us -> 141 us (0.89)
  Pallas kernels: 143 us -> 131 us
  local copies, waits for them, and re-layouts: 11.8 us -> 8.38 us
  other arithmetic: 3.18 us -> 0 us
    pallas_call x1, Pallas kernels: 137 us -> 126 us  [exchange_and_contract(): pl.pallas_call(functools.partial(main_kernel, nz), out_shape=jax.ShapeDty...]
    unnamed x0 -> x7, local copies, waits for them, and re-layouts: none -> 8.38 us
    transpose x1 -> x0, local copies, waits for them, and re-layouts: 5.25 us -> none  [per_device(): jnp.transpose(blocks, (1, 2, 3, 0, 4)).reshape(1, sinks, 2, m, nz * width)]
    reshape x1 -> x0, local copies, waits for them, and re-layouts: 5.22 us -> none  [per_device(): jnp.transpose(blocks, (1, 2, 3, 0, 4)).reshape(1, sinks, 2, m, nz * width)]
    select_n x3 -> x0, other arithmetic: 2.52 us -> none  [the longest x1 1.23 us: per_device(): jnp.where(slice_times[None, :] < source_times[:, None], -1.0, 1.0)]
where the time goes in v1:
time: 141 us; the launch traced here: 139 us
  Pallas kernels  131 us (93%)
  local copies, waits for them, and re-layouts  8.38 us (6%)
    pallas_call x1, Pallas kernels, exchange_and_contract(): pl.pallas_call(functools.partial(main_kernel, nz), out_shape=jax.ShapeDty...  126 us
    unnamed x7, local copies, waits for them, and re-layouts  8.38 us
    pallas_call x1, Pallas kernels, choose(): pl.pallas_call(choose_kernel, grid_spec=pltpu.PrefetchScalarGridSpec(num_...  5.17 us

profile of v1, /device:TPU:1, one launch (start us, length us, event | category | flops | bytes accessed | tf_op | source)
XLA Modules:
  0.0 139.2 jit_solution(9718182390270608260)
XLA Ops:
  0.0 5.2 %shard_map.55 = (f32[3,2,128,512]{3,2,1,0:T(8,128)}, f32[3,2,16,512]{3,2,1,0:T(8,128)}, f32[3,2,2,64,512]{4,3,2,1,0:T(8,128)}) custom-call(s32[3]{0:T(128)} %ins.1, s32[2]{0:T(128)} %start.1, f32[1,8,2,128,512]{4,3,2,1,0:T(8,128)} %left_ref.1, f32[8,2,16,512]{3,2,1,0:T(8,128)} %vertex_ref.1, f32[8,2,2,64,512]{4,3,2,1,0:T(8,128)} %bitcast.3), custom_call_target="tpu_custom_call" | custom-call | tf_op jit(solution)/shard_map/pallas_call | solution.py:36
  5.2 0.0 copy-start
  5.2 1.4 %copy-done = f32[3,2,128,512]{3,2,1,0:T(8,128)S(1)} copy-done((f32[3,2,128,512]{3,2,1,0:T(8,128)S(1)}, f32[3,2,128,512]{3,2,1,0:T(8,128)}, u32[]{:S(2)}) %copy-start) | copy-done | bytes 1572888
  6.6 0.0 copy-start.1
  6.6 1.4 %copy-done.1 = f32[3,2,2,64,512]{4,3,2,1,0:T(8,128)S(1)} copy-done((f32[3,2,2,64,512]{4,3,2,1,0:T(8,128)S(1)}, f32[3,2,2,64,512]{4,3,2,1,0:T(8,128)}, u32[]{:S(2)}) %copy-start.1) | copy-done | bytes 1572888
  8.0 0.0 copy-start.2
  8.0 0.9 copy-done.2
  8.9 125.7 %shard_map.56 = f32[1,2,2,512,512]{4,3,2,1,0:T(8,128)} custom-call(f32[3,2,128,512]{3,2,1,0:T(8,128)S(1)} %copy-done, f32[3,2,16,512]{3,2,1,0:T(8,128)S(1)} %copy-done.2, f32[3,256,512]{2,1,0:T(8,128)S(1)} %bitcast.2), custom_call_target="tpu_custom_call" | custom-call | tf_op jit(solution)/shard_map/pallas_call | solution.py:319
  134.6 4.6 %copy.7 = f32[1,2,2,512,512]{4,3,2,1,0:T(8,128)} copy(f32[1,2,2,512,512]{4,3,2,1,0:T(8,128)} %shard_map.56) | data formatting | bytes 8388608
Async XLA Ops:
  5.2 1.4 %copy-start = (f32[3,2,128,512]{3,2,1,0:T(8,128)S(1)}, f32[3,2,128,512]{3,2,1,0:T(8,128)}, u32[]{:S(2)}) copy-start(f32[3,2,128,512]{3,2,1,0:T(8,128)} %get-tuple-element.8.l_ref) | copy-start | bytes 4718596
  6.6 1.4 %copy-start.1 = (f32[3,2,2,64,512]{4,3,2,1,0:T(8,128)S(1)}, f32[3,2,2,64,512]{4,3,2,1,0:T(8,128)}, u32[]{:S(2)}) copy-start(f32[3,2,2,64,512]{4,3,2,1,0:T(8,128)} %get-tuple-element.10) | copy-start | bytes 4718596
  8.0 0.9 copy-start.2

commit v2 on v1

--- a/solution.py
+++ b/solution.py
@@ -14,18 +14,35 @@
 BF16 = jnp.bfloat16
 
 
-def choose_kernel(ins, start, left_ref, vertex_ref, right_ref, l_ref, v_ref, r_ref):
-    k = pl.program_id(0)
-    sinks = right_ref.shape[1]
-    slice_time = ins[k] * (LT // NS)
-    source_time = lax.rem(start[0] + lax.axis_index("row"), LT)
-    l_ref[0] = left_ref[0, 0] * jnp.where(slice_time < source_time, -1.0, 1.0).astype(F32)
-    v_ref[0] = vertex_ref[0]
-    for u in range(sinks):
-        sink_time = lax.rem(start[1] + lax.axis_index("col") * sinks + u, LT)
-        sign = jnp.where(sink_time < slice_time, -1.0, 1.0).astype(F32)
-        for part in range(2):
-            r_ref[0, part, u] = right_ref[0, u, part] * sign
+def choose_kernel(ins, start, left_ref, vertex_ref, right_ref, l_ref, v_ref, r_ref, sems):
+    count, sinks, cols = l_ref.shape[0], right_ref.shape[1], right_ref.shape[3]
+
+    def rows(part, u):
+        return pl.ds((part * sinks + u) * cols, cols)
+
+    def copies(k):
+        yield pltpu.make_async_copy(vertex_ref.at[ins[k]], v_ref.at[k], sems.at[k, 0])
+        yield pltpu.make_async_copy(left_ref.at[0, ins[k]], l_ref.at[k], sems.at[k, 1])
+        for u in range(sinks):
+            for part in range(2):
+                yield pltpu.make_async_copy(
+                    right_ref.at[ins[k], u, part], r_ref.at[k, rows(part, u)], sems.at[k, 2 + 2 * u + part]
+                )
+
+    for k in range(count):
+        for copy in copies(k):
+            copy.start()
+    for k in range(count):
+        for copy in copies(k):
+            copy.wait()
+        slice_time = ins[k] * (LT // NS)
+        source_time = lax.rem(start[0] + lax.axis_index("row"), LT)
+        l_ref[k] = l_ref[k] * jnp.where(slice_time < source_time, -1.0, 1.0).astype(F32)
+        for u in range(sinks):
+            sink_time = lax.rem(start[1] + lax.axis_index("col") * sinks + u, LT)
+            sign = jnp.where(sink_time < slice_time, -1.0, 1.0).astype(F32)
+            for part in range(2):
+                r_ref[k, rows(part, u), :] = r_ref[k, rows(part, u), :] * sign
 
 
 def choose(left_prop, vertex, right_t, insertions, window_start):
@@ -33,27 +50,18 @@
     _, _, _, lrows, m = left_prop.shape
     vrows = vertex.shape[2]
     sinks, cols = right_t.shape[1], right_t.shape[3]
+    smem = pl.BlockSpec(memory_space=pltpu.SMEM)
+    hbm = pl.BlockSpec(memory_space=pl.ANY)
     return pl.pallas_call(
         choose_kernel,
-        grid_spec=pltpu.PrefetchScalarGridSpec(
-            num_scalar_prefetch=2,
-            grid=(count,),
-            in_specs=[
-                pl.BlockSpec((1, 1, 2, lrows, m), lambda k, i, *_: (0, i[k], 0, 0, 0)),
-                pl.BlockSpec((1, 2, vrows, m), lambda k, i, *_: (i[k], 0, 0, 0)),
-                pl.BlockSpec((1, sinks, 2, cols, m), lambda k, i, *_: (i[k], 0, 0, 0, 0)),
-            ],
-            out_specs=[
-                pl.BlockSpec((1, 2, lrows, m), lambda k, *_: (k, 0, 0, 0)),
-                pl.BlockSpec((1, 2, vrows, m), lambda k, *_: (k, 0, 0, 0)),
-                pl.BlockSpec((1, 2, sinks, cols, m), lambda k, *_: (k, 0, 0, 0, 0)),
-            ],
-        ),
+        in_specs=[smem, smem, hbm, hbm, hbm],
+        out_specs=[pl.BlockSpec(memory_space=pltpu.VMEM)] * 3,
         out_shape=[
-            jax.ShapeDtypeStruct((count, 2, lrows, m), F32),
-            jax.ShapeDtypeStruct((count, 2, vrows, m), F32),
-            jax.ShapeDtypeStruct((count, 2, sinks, cols, m), F32),
+            pltpu.VMEM((count, 2, lrows, m), F32),
+            pltpu.VMEM((count, 2, vrows, m), F32),
+            pltpu.VMEM((count, 2 * sinks * cols, m), F32),
         ],
+        scratch_shapes=[pltpu.SemaphoreType.DMA((count, 2 + 2 * sinks))],
     )(insertions, window_start, left_prop, vertex, right_t)
 
 
@@ -217,7 +225,7 @@
 
     def split_lv(cs, k, part):
         high, low = halves(lv_all[cs, k, part])
-        at = pl.ds(pl.multiple_of(part * m + cs * lrows, lrows), lrows)
+        at = pl.ds(pl.multiple_of((2 * cs + part) * lrows, lrows), lrows)
         lv_high[k, at, :] = high
         lv_low[k, at, :] = low
 
@@ -233,11 +241,60 @@
             lv_pass(0, 0, k, part, c, to_x)
             lv_pass(1, 0, k, part, c, to_y)
 
-    r_step(1)
+    def sibling_step(d):
+        for zs, ok in ((z, None),) if d == 0 else tuple((hop[2], hop[3]) for hop in hops[d]):
+            for k in range(count):
+                src = lambda zs=zs, k=k: (r_all.at[2 * zs + 1 - h, k], r_recv.at[2 * zs + 1 - h, k])
+                if ok is None:
+                    arrived(*src())
+                else:
+                    pl.when(ok)(lambda src=src: arrived(*src()))
+
+    def store(q, cs, product):
+        at = pl.ds(pl.multiple_of(cs * lrows, lrows), lrows)
+        lanes = pl.ds(pl.multiple_of(q * 2 * cols, 2 * cols), 2 * cols)
+        real = [p[:lrows, :half] - p[lrows:, half:] for p in product]
+        imag = [p[:lrows, half:] + p[lrows:, :half] for p in product]
+        for u in range(sinks):
+            cut = slice(u * cols, (u + 1) * cols)
+            out_ref[0, u, 0, at, lanes] = jnp.concatenate([real[0][:, cut], real[1][:, cut]], axis=1)
+            out_ref[0, u, 1, at, lanes] = jnp.concatenate([imag[0][:, cut], imag[1][:, cut]], axis=1)
+
+    def times(k, at, yh, yl):
+        high = lv_high[k, at, :]
+        return dot_nt(high, yh) + dot_nt(lv_low[k, at, :], yh) + dot_nt(high, yl)
+
+    def contract(sources, first, last):
+        def chip(i, carry):
+            q = z + (i + 1) // 2 * (1 - 2 * lax.rem(i, 2))
+
+            @pl.when(jnp.logical_and(q >= 0, q < nz))
+            def _():
+                for j in range(2):
+                    for k in range(count):
+                        yh, yl = halves(r_all[2 * q + j, k])
+                        for cs in sources:
+                            at = pl.ds(pl.multiple_of(cs * 2 * lrows, 2 * lrows), 2 * lrows)
+                            if k == 0:
+                                acc[j, at, :] = times(k, at, yh, yl)
+                            else:
+                                acc[j, at, :] += times(k, at, yh, yl)
+                for cs in sources:
+                    at = pl.ds(pl.multiple_of(cs * 2 * lrows, 2 * lrows), 2 * lrows)
+                    store(q, cs, [acc[0, at, :], acc[1, at, :]])
+
+            return carry
+
+        lax.fori_loop(first, last, chip, 0)
 
     for k in range(count):
         for part in range(2):
             split_lv(c, k, part)
+    r_step(1)
+    sibling_step(0)
+    contract([c], 0, 1)
+    sibling_step(1)
+    contract([c], 1, 3)
     for k in range(count):
         for part in range(2):
             arrived(lv_piece(cx, k, part), lv_recv.at[cx, k, part])
@@ -250,20 +307,23 @@
             split_lv(cy, k, part)
     for d in range(2, nz - 1):
         r_step(d)
+    contract([cx, cy], 0, 3)
+    for d in range(2, nz - 1):
+        sibling_step(d)
+    contract([c, cx, cy], 3, 2 * nz - 3)
     for k in range(count):
         for part in range(2):
             arrived(lv_piece(cd, k, part), lv_recv.at[cd, k, part])
             split_lv(cd, k, part)
-
-    def chip(i, carry):
-        d = (i + 1) // 2
-        q = z + d * (1 - 2 * lax.rem(i, 2))
+    contract([cd], 0, 2 * nz - 3)
+
+    def farthest(i, carry):
+        q = z + (nz - 1) * (1 - 2 * i)
 
         @pl.when(jnp.logical_and(q >= 0, q < nz))
         def _():
             for k in range(count):
-                if nz > 2:
-                    pl.when(d == nz - 1)(lambda k=k: r_step(nz - 1, [k]))
+                r_step(nz - 1, [k])
 
                 def one(n, carry, k=k):
                     j = h + n * (1 - 2 * h)
@@ -273,33 +333,22 @@
                         arrived(r_all.at[2 * q + j, k], r_recv.at[2 * q + j, k])
 
                     yh, yl = halves(r_all[2 * q + j, k])
-                    for part in range(2):
-                        at = pl.ds(part * m, m)
-                        p = (
-                            dot_nt(lv_high[k, at, :], yh)
-                            + dot_nt(lv_low[k, at, :], yh)
-                            + dot_nt(lv_high[k, at, :], yl)
-                        )
+                    for cs in range(0, ncol, 2):
+                        at = pl.ds(cs * 2 * lrows, 4 * lrows)
                         if k == 0:
-                            acc[j, at, :] = p
+                            acc[j, at, :] = times(k, at, yh, yl)
                         else:
-                            acc[j, at, :] += p
+                            acc[j, at, :] += times(k, at, yh, yl)
                     return carry
 
                 lax.fori_loop(0, 2, one, 0)
-            real, imag = [], []
-            for j in range(2):
-                real.append(acc[j, pl.ds(0, m), pl.ds(0, half)] - acc[j, pl.ds(m, m), pl.ds(half, half)])
-                imag.append(acc[j, pl.ds(0, m), pl.ds(half, half)] + acc[j, pl.ds(m, m), pl.ds(0, half)])
-            lanes = pl.ds(pl.multiple_of(q * 2 * cols, 2 * cols), 2 * cols)
-            for u in range(sinks):
-                cut = slice(u * cols, (u + 1) * cols)
-                out_ref[0, u, 0, :, lanes] = jnp.concatenate([real[0][:, cut], real[1][:, cut]], axis=1)
-                out_ref[0, u, 1, :, lanes] = jnp.concatenate([imag[0][:, cut], imag[1][:, cut]], axis=1)
+            for cs in range(ncol):
+                at = pl.ds(cs * 2 * lrows, 2 * lrows)
+                store(q, cs, [acc[0, at, :], acc[1, at, :]])
 
         return carry
 
-    lax.fori_loop(0, 2 * nz - 1, chip, 0)
+    lax.fori_loop(0, 2, farthest, 0)
 
     for when, make in pending:
         if when is None:
@@ -308,17 +357,17 @@
             pl.when(when)(lambda make=make: make().wait_send())
 
 
-def exchange_and_contract(nrow, ncol, chosen_left, chosen_vertex, chosen_right):
+def exchange_and_contract(nrow, ncol, sinks, chosen_left, chosen_vertex, chosen_right):
     count, _, lrows, m = chosen_left.shape
     vrows = chosen_vertex.shape[2]
-    sinks, cols = chosen_right.shape[2], chosen_right.shape[3]
-    rrows = 2 * sinks * cols
+    rrows = chosen_right.shape[1]
+    cols = rrows // (2 * sinks)
     nz = nrow // 2
     dma = pltpu.SemaphoreType.DMA
     vmem = pl.BlockSpec(memory_space=pltpu.VMEM)
     return pl.pallas_call(
         functools.partial(main_kernel, nz),
-        out_shape=jax.ShapeDtypeStruct((1, sinks, 2, m, nrow * cols), F32),
+        out_shape=pltpu.VMEM((1, sinks, 2, m, nrow * cols), F32),
         in_specs=[vmem, vmem, vmem],
         out_specs=vmem,
         scratch_shapes=[
@@ -337,9 +386,9 @@
             dma((ncol, count, 2)),
         ],
         compiler_params=pltpu.CompilerParams(
-            collective_id=0, has_side_effects=True, vmem_limit_bytes=48 * 1024 * 1024
+            collective_id=0, has_side_effects=True, vmem_limit_bytes=42 * 1024 * 1024
         ),
-    )(chosen_left, chosen_vertex, chosen_right.reshape(count, rrows, m))
+    )(chosen_left, chosen_vertex, chosen_right)
 
 
 def complex_product(first, second):
@@ -382,14 +431,14 @@
     source_count = left_prop.shape[0]
     lrows, m = left_prop.shape[3:]
     fits = (
-        source_count == 1 and ncol == 4 and nrow % 2 == 0 and nrow >= 4 and vertex.shape[2] % 8 == 0
+        source_count == 1 and ncol == 4 and nrow % 2 == 0 and nrow >= 6 and vertex.shape[2] % 8 == 0
         and lrows % 16 == 0 and m % 128 == 0 and 2 * right_prop.shape[4] == 128
         and right_prop.shape[1] * right_prop.shape[4] == 128
     )
     if not fits:
         return general(left_prop, vertex, right_prop, insertions, window_start)
     chosen = choose(left_prop, vertex, jnp.swapaxes(right_prop, 3, 4), insertions, window_start)
-    return exchange_and_contract(nrow, ncol, *chosen)
+    return exchange_and_contract(nrow, ncol, right_prop.shape[1], *chosen)
 
 
 def solution(mesh):

time: 141 us -> 129 us (0.915)
  local copies, waits for them, and re-layouts: 8.38 us -> 2.02 us
  Pallas kernels: 131 us -> 127 us
    unnamed x7 -> x1, local copies, waits for them, and re-layouts: 8.38 us -> 2.02 us
    pallas_call x2, Pallas kernels: 131 us -> 127 us  [the longest x1 124 us: exchange_and_contract(): pl.pallas_call(functools.partial(main_kernel, nz), out_shape=pltpu.VMEM((...]
where the time goes in v2:
time: 129 us
  Pallas kernels  127 us (98%)
  local copies, waits for them, and re-layouts  2.02 us (2%)
    pallas_call x1, Pallas kernels, exchange_and_contract(): pl.pallas_call(functools.partial(main_kernel, nz), out_shape=pltpu.VMEM((...  124 us
    pallas_call x1, Pallas kernels, choose(): pl.pallas_call(choose_kernel, in_specs=[smem, smem, hbm, hbm, hbm], out_s...  2.79 us

profile of v2, /device:TPU:1, one launch (start us, length us, event | category | flops | bytes accessed | tf_op | source)
XLA Modules:
  0.0 128.6 jit_solution(11538492671340372803)
XLA Ops:
  0.0 2.8 %shard_map.55 = (f32[3,2,128,512]{3,2,1,0:T(8,128)S(1)}, f32[3,2,16,512]{3,2,1,0:T(8,128)S(1)}, f32[3,256,512]{2,1,0:T(8,128)S(1)}) custom-call(s32[3]{0:T(128)} %ins.1, s32[2]{0:T(128)} %start.1, f32[1,8,2,128,512]{4,3,2,1,0:T(8,128)} %left_ref.1, f32[8,2,16,512]{3,2,1,0:T(8,128)} %vertex_ref.1, f32[8,2,2,64,512]{4,3,2,1,0:T(8,128)} %bitcast.1), custom_call_target="tpu_custom_call" | custom-call | tf_op jit(solution)/shard_map/pallas_call | solution.py:55
  2.8 123.8 %shard_map.56 = f32[1,2,2,512,512]{4,3,2,1,0:T(8,128)S(1)} custom-call(f32[3,2,128,512]{3,2,1,0:T(8,128)S(1)} %get-tuple-element.8.l_ref, f32[3,2,16,512]{3,2,1,0:T(8,128)S(1)} %get-tuple-element.9.v_ref, f32[3,256,512]{2,1,0:T(8,128)S(1)} %get-tuple-element.10.r_ref), custom_call_target="tpu_custom_call" | custom-call | tf_op jit(solution)/shard_map/pallas_call | solution.py:368
  126.6 2.0 %copy.7 = f32[1,2,2,512,512]{4,3,2,1,0:T(8,128)} copy(f32[1,2,2,512,512]{4,3,2,1,0:T(8,128)S(1)} %shard_map.56) | data formatting | bytes 8388608
